TPU v7x, 256 devices: a whole 4x4x8 slice. The times are simulated.
256 devices in a mesh: wide: 128 (over y, x_hi, z, core), narrow: 2 (over x_lo).
Axes of the slice: x: 4 (x_hi: 2, x_lo: 2; x = x_hi * 2 + x_lo), y: 4, z: 8, core: 2. Of those that a mesh axis runs over, the one named last changes fastest.
Arguments:
- positions: float32 [3, 65536], P(None, 'wide'), may hold values from -6 to 6
- velocities: float32 [3, 65536], P(None, 'wide'), may hold values from -6 to 6
- accelerations: float32 [3, 65536], P(None, 'wide'), may hold values from -6 to 6
- jerks: float32 [3, 65536], P(None, 'wide'), may hold values from -6 to 6
- snaps: float32 [3, 65536], P(None, 'wide'), may hold values from -36 to 36
- masses: float32 [65536], P('wide'), may hold values from 0.5 to 2
Outputs:
- new_positions: float32 [3, 65536], P(None, 'wide')
- new_velocities: float32 [3, 65536], P(None, 'wide')
- new_accelerations: float32 [3, 65536], P(None, 'wide')
- new_jerks: float32 [3, 65536], P(None, 'wide')
- new_snaps: float32 [3, 65536], P(None, 'wide')
- crackle_step: float32 [3, 65536], P(None, 'wide')
All inputs are finite; a program needn't handle non-finite values.
Results may differ from a plain program's by a relative error of at most 0.00026.
Values sent between devices are 32-bit elements; how exact they have to be, the bound alone decides.
A program may use at most 64 MiB of HBM per device.

v0:
```python
import math

import jax
import jax.numpy as jnp
from jax import lax
from jax.sharding import PartitionSpec as P

softening = 0.01
time_step = 0.0625


def predict(positions, velocities, accelerations, jerks, snaps):
    pred_x = (
        positions
        + time_step * velocities
        + time_step * time_step / 2.0 * accelerations
        + time_step**3 / 6.0 * jerks
        + time_step**4 / 24.0 * snaps
    )
    pred_v = (
        velocities
        + time_step * accelerations
        + time_step * time_step / 2.0 * jerks
        + time_step**3 / 6.0 * snaps
    )
    pred_a = accelerations + time_step * jerks + time_step * time_step / 2.0 * snaps
    return (pred_x, pred_v, pred_a)


def pair_forces(targets, sources):
    separation = sources[0:3, None, :] - targets[0:3, :, None]
    relative_vel = sources[3:6, None, :] - targets[3:6, :, None]
    relative_acc = sources[6:9, None, :] - targets[6:9, :, None]
    dist_sq = jnp.sum(separation * separation, axis=0) + softening
    inverse_sq = 1.0 / dist_sq
    strength = sources[9][None, :] * inverse_sq * jnp.sqrt(inverse_sq)
    radial = jnp.sum(separation * relative_vel, axis=0) * inverse_sq
    curving = (
        jnp.sum(relative_vel * relative_vel, axis=0) + jnp.sum(separation * relative_acc, axis=0)
    ) * inverse_sq + radial * radial
    accel_pair = strength * separation
    jerk_pair = strength * relative_vel - 3.0 * radial * accel_pair
    snap_pair = strength * relative_acc - 6.0 * radial * jerk_pair - 3.0 * curving * accel_pair
    return jnp.concatenate(
        [jnp.sum(accel_pair, axis=-1), jnp.sum(jerk_pair, axis=-1), jnp.sum(snap_pair, axis=-1)],
        axis=0,
    )


def sum_sources(targets, piece):
    count_src = piece.shape[1]
    block_size = math.gcd(count_src, 1024)
    blocks = piece.reshape(10, count_src // block_size, block_size).transpose(1, 0, 2)

    def add_block(carry, block):
        return (carry + pair_forces(targets, block), None)

    total, _ = lax.scan(add_block, jnp.zeros((9, targets.shape[1]), jnp.float32), blocks)
    return total


def correct(positions, velocities, accelerations, jerks, snaps, forces):
    new_acc = forces[0:3]
    new_jerk = forces[3:6]
    new_snap = forces[6:9]
    new_vel = (
        velocities
        + time_step / 2.0 * (new_acc + accelerations)
        - time_step * time_step / 10.0 * (new_jerk - jerks)
        + time_step**3 / 120.0 * (new_snap + snaps)
    )
    new_pos = (
        positions
        + time_step / 2.0 * (new_vel + velocities)
        - time_step * time_step / 10.0 * (new_acc - accelerations)
        + time_step**3 / 120.0 * (new_jerk + jerks)
    )
    first = new_acc - accelerations - time_step * jerks - time_step * time_step / 2.0 * snaps
    second = time_step * (new_jerk - jerks - time_step * snaps)
    third = time_step * time_step * (new_snap - snaps)
    crackle = 60.0 * first - 36.0 * second + 9.0 * third
    return (new_pos, new_vel, new_acc, new_jerk, new_snap, crackle)


def halves_of(arrays, start, count):
    return tuple((lax.dynamic_slice_in_dim(item, start, count, 1) for item in arrays))


def shards(positions, velocities, accelerations, jerks, snaps, masses):
    local_count = positions.shape[1]
    star_total = local_count * lax.axis_size("wide")
    half_count = local_count // 2
    narrow_index = lax.axis_index("narrow")
    half_start = narrow_index * half_count
    pred_x, pred_v, pred_a = predict(positions, velocities, accelerations, jerks, snaps)
    source = jnp.concatenate([pred_x, pred_v, pred_a, (masses / star_total)[None, :]], axis=0)
    targets = source[0:9]
    start_state = (positions, velocities, accelerations, jerks, snaps)
    own_targets = lax.dynamic_slice_in_dim(targets, half_start, half_count, 1)
    forces = sum_sources(own_targets, lax.all_gather(source, "wide", axis=1, tiled=True))
    state_half = halves_of(start_state, half_start, half_count)
    results = correct(
        state_half[0], state_half[1], state_half[2], state_half[3], state_half[4], forces
    )
    new_pos, new_vel, new_acc, new_jerk, new_snap, crackle = results
    return (
        lax.all_gather(new_pos, "narrow", axis=1, tiled=True),
        lax.all_gather(new_vel, "narrow", axis=1, tiled=True),
        lax.all_gather(new_acc, "narrow", axis=1, tiled=True),
        lax.all_gather(new_jerk, "narrow", axis=1, tiled=True),
        lax.all_gather(new_snap, "narrow", axis=1, tiled=True),
        lax.all_gather(crackle, "narrow", axis=1, tiled=True),
    )


def solution(mesh):
    return jax.shard_map(
        shards,
        mesh=mesh,
        in_specs=(
            P(None, "wide"),
            P(None, "wide"),
            P(None, "wide"),
            P(None, "wide"),
            P(None, "wide"),
            P("wide"),
        ),
        out_specs=(
            P(None, "wide"),
            P(None, "wide"),
            P(None, "wide"),
            P(None, "wide"),
            P(None, "wide"),
            P(None, "wide"),
        ),
        check_vma=False,
    )
```

profile of v0, /device:TPU:2, one launch (start us, length us, event | category | flops | bytes accessed | tf_op | source)
XLA Modules:
  0.0 757.1 jit_solution(16952772460760008505)
XLA Ops:
  9.4 123.6 %all-gather.2.cloned.1.call-done = f32[10,65536]{1,0:T(8,128)} async-done(((f32[10,512]{1,0:T(8,128)}), f32[10,65536]{1,0:T(8,128)}) %all-gather.2.cloned.1.call-update) | async-done | bytes 2621456 | tf_op jit(solution)/shard_map/all_gather | solution.py:100
  133.0 4.6 copy.14
  138.0 3.5 copy.16
  141.5 579.1 %while.11 = (s32[]{:T(128)}, f32[9,256]{1,0:T(8,128)S(1)}, f32[64,10,1024]{2,1,0:T(8,128)}, f32[9,256]{1,0:T(8,128)S(1)}, s32[]{:T(128)}, /*index=5*/s32[]{:T(128)}, s32[]{}, s32[]{}, s32[]{}) while((s32[]{:T(128)}, f32[9,256]{1,0:T(8,128)S(1)}, f32[64,10,1024]{2,1,0:T(8,128)}, f32[9,256]{1,0:T(8,128)S(1)}, s32[]{:T(128)}, ...), condition=%wide.region_8.9_spmd.clone, body=%wide.region_0.8_spmd.clone.sunk | while | flops 22551300 | bytes 17010844 | solution.py:58
  142.5 2.7 fusion.20
  151.5 2.7 fusion.20
  160.6 2.7 fusion.20
  169.6 2.7 fusion.20
  178.7 2.7 fusion.20
  187.7 2.7 fusion.20
  196.8 2.7 fusion.20
  205.8 2.7 fusion.20
  214.9 2.7 fusion.20
  223.9 2.7 fusion.20
  233.0 2.7 fusion.20
  242.0 2.7 fusion.20
  251.1 2.7 fusion.20
  260.1 2.7 fusion.20
  269.2 2.7 fusion.20
  278.2 2.7 fusion.20
  287.3 2.7 fusion.20
  296.3 2.7 fusion.20
  305.4 2.7 fusion.20
  314.4 2.7 fusion.20
  323.5 2.7 fusion.20
  332.5 2.7 fusion.20
  341.6 2.7 fusion.20
  350.6 2.7 fusion.20
  359.7 2.7 fusion.20
  368.7 2.7 fusion.20
  377.8 2.7 fusion.20
  386.8 2.7 fusion.20
  395.9 2.7 fusion.20
  404.9 2.7 fusion.20
  414.0 2.7 fusion.20
  423.0 2.7 fusion.20
  432.1 2.7 fusion.20
  441.1 2.7 fusion.20
  450.2 2.7 fusion.20
  459.2 2.7 fusion.20
  468.3 2.7 fusion.20
  640.2 2.7 fusion.20
  720.7 4.3 all_gather.22
  725.1 4.3 all_gather.23
  729.4 4.3 all_gather.24
  733.7 4.3 all_gather.25
  738.0 4.3 all_gather.26
  742.4 4.3 all_gather.27
  (435 shorter events, 480.1 us)
Async XLA Ops:
  7.2 125.8 %all-gather.2.cloned.1.call-start = ((), (), s32[]{:S(2)}) async-start(), calls=%async_computation | async-start | bytes 4227072 | tf_op jit(solution)/shard_map/all_gather | solution.py:100
  141.5 579.2 %copy-start = (f32[3,512]{1,0:T(4,128)S(1)}, f32[3,512]{1,0:T(4,128)}, u32[]{:S(2)}) copy-start(f32[3,512]{1,0:T(4,128)} %param.8) | copy-start | bytes 18436
  141.5 579.2 %copy-start.1 = (f32[3,512]{1,0:T(4,128)S(1)}, f32[3,512]{1,0:T(4,128)}, u32[]{:S(2)}) copy-start(f32[3,512]{1,0:T(4,128)} %param.9) | copy-start | bytes 18436
  141.5 579.2 %copy-start.2 = (f32[3,512]{1,0:T(4,128)S(1)}, f32[3,512]{1,0:T(4,128)}, u32[]{:S(2)}) copy-start(f32[3,512]{1,0:T(4,128)} %param.11) | copy-start | bytes 18436
  141.5 579.2 %copy-start.3 = (f32[3,512]{1,0:T(4,128)S(1)}, f32[3,512]{1,0:T(4,128)}, u32[]{:S(2)}) copy-start(f32[3,512]{1,0:T(4,128)} %param.10) | copy-start | bytes 18436
  141.5 579.2 %copy-start.4 = (f32[3,512]{1,0:T(4,128)S(1)}, f32[3,512]{1,0:T(4,128)}, u32[]{:S(2)}) copy-start(f32[3,512]{1,0:T(4,128)} %param.12) | copy-start | bytes 18436
Sparse Core Ops, SparseCore 0:
  11.8 121.1 all-gather.1
where the time goes:
time: 768 us; the launch traced here: 757 us
  other arithmetic  467 us (61%)
  waiting for transfers between devices  124 us (16%)
  local copies, waits for them, and re-layouts  124 us (16%)
  blocking collectives  26 us (3%)
  between operations  14.1 us (2%)
    reduce_sum x64, other arithmetic, pair_forces(): dist_sq = jnp.sum(separation * separation, axis=0) + softening  172 us
    reduce_sum x64, other arithmetic, pair_forces(): jnp.sum(jerk_pair, axis=-1)  158 us
    mul x64, other arithmetic, pair_forces(): 6.0 * radial * jerk_pair  134 us
    all_gather x1, waiting for transfers between devices, shards(): lax.all_gather(source, 'wide', axis=1, tiled=True)  124 us
    sub x64, local copies, waits for them, and re-layouts, pair_forces(): relative_vel = sources[3:6, None, :] - targets[3:6, :, None]  62.4 us
    slice x64, local copies, waits for them, and re-layouts, pair_forces(): strength = sources[9][None, :] * inverse_sq * jnp.sqrt(inverse_sq)  48.9 us
  transfers between devices with their start and end apart: 1, of which 1 were waited for; matrix products, arithmetic and copies ran while one was open for 0% of the time, Pallas kernels for 0%

commit v1 on v0

v1 whole, which is shorter than its diff:
```python
import functools

import jax
import jax.numpy as jnp
from jax import lax
from jax.experimental import pallas as pl
from jax.experimental.pallas import tpu as pltpu
from jax.sharding import PartitionSpec as P

softening = 0.01
time_step = 0.0625

bf16 = jnp.bfloat16
f32 = jnp.float32
f8 = jnp.float8_e4m3fn
MESH = pl.DeviceIdType.MESH

CORES, NZ, NX, NY = 2, 8, 2, 4
BLOCKS = CORES * NZ * NX * NY
CHUNK = 2
PARTS = 2
STEP = CHUNK * PARTS
TILE = 256

Q_SCALE = 2.0**-4
P_SCALE = 2.0**-10.5
G_SCALE = 0.2 * 2.0**-17
W_BACK = 2.0**-6
C1_BACK = 2.0**0.5
C2_BACK = 2.0**7


def predict(positions, velocities, accelerations, jerks, snaps):
    pred_x = (
        positions
        + time_step * velocities
        + time_step * time_step / 2.0 * accelerations
        + time_step**3 / 6.0 * jerks
        + time_step**4 / 24.0 * snaps
    )
    pred_v = (
        velocities
        + time_step * accelerations
        + time_step * time_step / 2.0 * jerks
        + time_step**3 / 6.0 * snaps
    )
    pred_a = accelerations + time_step * jerks + time_step * time_step / 2.0 * snaps
    return (pred_x, pred_v, pred_a)


def correct(positions, velocities, accelerations, jerks, snaps, forces):
    new_acc = forces[0:3]
    new_jerk = forces[3:6]
    new_snap = forces[6:9]
    new_vel = (
        velocities
        + time_step / 2.0 * (new_acc + accelerations)
        - time_step * time_step / 10.0 * (new_jerk - jerks)
        + time_step**3 / 120.0 * (new_snap + snaps)
    )
    new_pos = (
        positions
        + time_step / 2.0 * (new_vel + velocities)
        - time_step * time_step / 10.0 * (new_acc - accelerations)
        + time_step**3 / 120.0 * (new_jerk + jerks)
    )
    first = new_acc - accelerations - time_step * jerks - time_step * time_step / 2.0 * snaps
    second = time_step * (new_jerk - jerks - time_step * snaps)
    third = time_step * time_step * (new_snap - snaps)
    crackle = 60.0 * first - 36.0 * second + 9.0 * third
    return (new_pos, new_vel, new_acc, new_jerk, new_snap, crackle)


def transfers():
    plan = []

    def put(step, to, src, dst, count=1):
        plan.append((step, to, src, dst, count))

    for to, dst in (("core", 1), ("z+", 2), ("z-", 3), ("y+", 4), ("y-", 5), ("x", 17)):
        put(-1, to, 0, dst)
    put(0, "z+", 2, 8)
    put(0, "z-", 3, 9)
    put(0, "core", 2, 6, 2)
    put(0, "y+", 2, 19, 2)
    put(0, "y-", 2, 34, 2)
    put(0, "x", 2, 65, 2)
    put(0, "core", 4, 26)
    put(0, "core", 5, 41)
    put(0, "y+", 4, 49)
    put(0, "x", 4, 80)
    put(0, "x", 5, 96)
    put(1, "z+", 8, 12)
    put(1, "z-", 9, 13)
    put(1, "core", 8, 10, 2)
    put(1, "y+", 8, 21, 2)
    put(1, "y-", 8, 36, 2)
    put(1, "x", 8, 67, 2)
    put(2, "z+", 12, 16)
    put(2, "core", 12, 14, 2)
    put(2, "y+", 12, 23, 2)
    put(2, "y-", 12, 38, 2)
    put(2, "x", 12, 69, 2)
    put(3, "core", 16, 18)
    put(3, "y+", 16, 25)
    put(3, "y-", 16, 40)
    put(3, "x", 16, 71)
    put(3, "core", 17, 72)
    put(4, "y+", 19, 50, 3)
    put(5, "core", 19, 27, 7)
    put(5, "x", 19, 81, 7)
    put(5, "y-", 37, 53, 4)
    put(5, "core", 34, 42, 7)
    put(5, "x", 34, 97, 7)
    put(8, "core", 49, 57, 8)
    put(8, "x", 49, 112, 8)
    put(12, "core", 65, 73, 7)
    put(14, "core", 80, 88, 8)
    put(16, "core", 96, 104, 8)
    put(18, "core", 112, 120, 8)
    return plan


def waits(plan):
    due = []
    for _, _, _, dst, count in plan:
        use = max(-1, -((5 - dst) // STEP))
        for step, _, src, _, length in plan:
            if src < dst + count and dst < src + length:
                use = min(use, step)
        due.append(use)
    return due


def split3(value):
    high = value.astype(bf16)
    rest = value - high.astype(f32)
    middle = rest.astype(bf16)
    low = (rest - middle.astype(f32)).astype(bf16)
    return high, middle, low


def product(left, right, over_left):
    return lax.dot_general(
        left, right, (((over_left,), (0,)), ((), ())), preferred_element_type=f32
    )


def source_rows(block):
    high, middle, low = split3(block)
    return jnp.concatenate([high, high, high, middle, middle, low], axis=0)


def sum_rows(block):
    weighed = block * block[12:13]
    fine = jnp.concatenate(split3(weighed), axis=0)
    high = weighed.astype(f8)
    rest = (weighed - high.astype(f32)).astype(f8)
    coarse = jnp.concatenate([high.astype(f32), rest.astype(f32)], axis=0).astype(f8)
    return fine, coarse


def forces_kernel(
    pos_ref, vel_ref, acc_ref, jerk_ref, snap_ref, mass_ref, out_ref,
    slots, own, feature, weights, pairs, total, total_low, part, other,
    send_sem, recv_sem, narrow_sem,
):
    wide, narrow = lax.axis_index("wide"), lax.axis_index("narrow")
    core, z = wide % CORES, (wide // CORES) % NZ
    x, y = (wide // (CORES * NZ)) % NX, wide // (CORES * NZ * NX)

    def index(y, x, z, core):
        return ((y * NX + x) * NZ + z) * CORES + core

    partner = {
        "core": {"wide": index(y, x, z, 1 - core)},
        "z+": {"wide": index(y, x, (z + 1) % NZ, core)},
        "z-": {"wide": index(y, x, (z + NZ - 1) % NZ, core)},
        "y+": {"wide": index((y + 1) % NY, x, z, core)},
        "y-": {"wide": index((y + NY - 1) % NY, x, z, core)},
        "x": {"wide": index(y, 1 - x, z, core)},
        "narrow": {"narrow": 1 - narrow},
    }
    barrier = pltpu.get_barrier_semaphore()
    for device in partner.values():
        pl.semaphore_signal(barrier, inc=1, device_id=device, device_id_type=MESH)

    star_x, star_v, star_a = predict(
        pos_ref[...], vel_ref[...], acc_ref[...], jerk_ref[...], snap_ref[...]
    )
    targets = star_x.shape[1]
    half = targets // 2
    xx = jnp.sum(star_x * star_x, axis=0, keepdims=True)
    xv = jnp.sum(star_x * star_v, axis=0, keepdims=True)
    vv = jnp.sum(star_v * star_v, axis=0, keepdims=True) + jnp.sum(
        star_x * star_a, axis=0, keepdims=True
    )
    one = jnp.ones_like(xx)
    own[...] = jnp.zeros_like(own)
    for row, value in (
        (0, star_x), (3, star_v), (6, star_a), (9, xx), (10, xv), (11, vv),
        (12, mass_ref[...]), (13, one),
    ):
        own[row : row + value.shape[0], :] = value
    start = pl.multiple_of(narrow * half, half)
    slots[0] = own[:, pl.ds(start, half)]
    pl.semaphore_wait(barrier, len(partner))

    plan = transfers()
    due = waits(plan)

    def copy(number):
        _, to, src, dst, count = plan[number]
        return pltpu.make_async_remote_copy(
            src_ref=slots.at[pl.ds(src, count)],
            dst_ref=slots.at[pl.ds(dst, count)],
            send_sem=send_sem.at[number],
            recv_sem=recv_sem.at[number],
            device_id=partner[to],
            device_id_type=MESH,
        )

    def exchange(step):
        for number in range(len(plan)):
            if due[number] == step and plan[number][0] < step:
                copy(number).wait_recv()
        for number in range(len(plan)):
            if plan[number][0] == step:
                copy(number).start()
        for number in range(len(plan)):
            if due[number] == step and plan[number][0] >= step:
                copy(number).wait_recv()

    for number in range(len(plan)):
        if plan[number][0] == -1:
            copy(number).start()

    feature[...] = jnp.zeros_like(feature)
    for kind, rows in enumerate((
        ((0, -2.0 * Q_SCALE * star_x), (9, Q_SCALE * one), (13, Q_SCALE * (xx + softening))),
        ((0, -P_SCALE * star_v), (3, -P_SCALE * star_x), (10, P_SCALE * one), (13, P_SCALE * xv)),
        (
            (0, -G_SCALE * star_a), (3, -2.0 * G_SCALE * star_v), (6, -G_SCALE * star_x),
            (11, G_SCALE * one), (13, G_SCALE * vv),
        ),
    )):
        for row, value in rows:
            feature[kind, row : row + value.shape[0], :] = value
        high, middle, low = split3(feature[kind])
        weights[kind] = jnp.concatenate([high, middle, low, high, middle, high], axis=0)

    total[...] = jnp.zeros_like(total)
    total_low[...] = jnp.zeros_like(total_low)

    def chunk_of(number):
        return jnp.concatenate([slots[number * CHUNK + u] for u in range(CHUNK)], axis=1)

    def forward(rows, parity, kind, tile):
        columns = slice(tile * TILE, (tile + 1) * TILE)
        pairs[parity, kind, :, columns] = product(rows, weights[kind, :, columns], 0)

    for number in range(len(plan)):
        if plan[number][0] == -1 and due[number] == -1:
            copy(number).wait_recv()
    rows = source_rows(chunk_of(0))
    for kind in range(3):
        for tile in range(targets // TILE):
            forward(rows, 0, kind, tile)

    steps = BLOCKS // STEP
    events = sorted(set([d for d in due if d >= 0] + [t[0] for t in plan if t[0] >= 0]))

    def branch(step, numbers):
        if len(numbers) <= 2:
            for number in numbers:
                pl.when(step == number)(functools.partial(exchange, number))
            return
        middle = len(numbers) // 2
        first, second = numbers[:middle], numbers[middle:]
        pl.when(step < second[0])(functools.partial(branch, step, first))
        pl.when(step >= second[0])(functools.partial(branch, step, second))

    def body(step, carry):
        branch(step, events)
        for parity in range(PARTS):
            chunk = step * PARTS + parity
            now, later = parity % 2, (parity + 1) % 2
            fine, coarse = sum_rows(chunk_of(chunk))
            ahead = source_rows(chunk_of(lax.min(chunk + 1, BLOCKS // CHUNK - 1)))
            work = [(kind, tile) for kind in range(3) for tile in range(targets // TILE)]
            units = [(b, tile) for b in range(CHUNK) for tile in range(targets // TILE)]
            done = 0
            for place, (b, tile) in enumerate(units):
                js = slice(b * half, (b + 1) * half)
                columns = slice(tile * TILE, (tile + 1) * TILE)
                q, p, g = [pairs[now, kind, js, columns] for kind in range(3)]
                root = lax.rsqrt(q)
                inverse = root * root
                w = inverse * root
                radial = p * inverse
                c1 = radial * w
                c2 = (w * inverse) * (p * radial - g)
                for kind, value in enumerate((w, c1, c2)):
                    high = value.astype(bf16)
                    low = (value - high.astype(f32)).astype(f8)
                    total[kind, :, columns] += product(fine[:, js], high, 1)
                    total_low[kind, :, columns] += product(coarse[:, js], low, 1)
                until = (place + 1) * len(work) // len(units)
                for kind, at in work[done:until]:
                    forward(ahead, later, kind, at)
                done = until
        return carry

    lax.fori_loop(0, steps, body, 0)

    sums = []
    for kind in range(3):
        sums.append(
            total[kind, 0:16] + total[kind, 16:32] + total[kind, 32:48]
            + total_low[kind, 0:16] + total_low[kind, 16:32]
        )
    sw, s1, s2 = sums
    share = 1.0 / (targets * BLOCKS)
    star_x, star_v, star_a = own[0:3, :], own[3:6, :], own[6:9, :]
    part[...] = jnp.zeros_like(part)
    part[0:3, :] = (W_BACK * share) * (sw[0:3] - star_x * sw[13:14])
    c1x = (C1_BACK * share) * (s1[0:3] - star_x * s1[13:14])
    part[3:6, :] = (W_BACK * share) * (sw[3:6] - star_v * sw[13:14]) - 3.0 * c1x
    part[6:9, :] = (
        (W_BACK * share) * (sw[6:9] - star_a * sw[13:14])
        - (6.0 * C1_BACK * share) * (s1[3:6] - star_v * s1[13:14])
        + (15.0 * C2_BACK * share) * (s2[0:3] - star_x * s2[13:14])
    )
    swap = pltpu.make_async_remote_copy(
        src_ref=part,
        dst_ref=other,
        send_sem=narrow_sem.at[0],
        recv_sem=narrow_sem.at[1],
        device_id=partner["narrow"],
        device_id_type=MESH,
    )
    swap.start()
    for number in range(len(plan)):
        copy(number).wait_send()
    swap.wait()
    out_ref[...] = part[...] + other[...]


def shards(positions, velocities, accelerations, jerks, snaps, masses):
    targets = positions.shape[1]
    half = targets // 2
    count = len(transfers())
    forces = pl.pallas_call(
        forces_kernel,
        out_shape=jax.ShapeDtypeStruct((16, targets), f32),
        in_specs=[pl.BlockSpec(memory_space=pltpu.VMEM)] * 6,
        out_specs=pl.BlockSpec(memory_space=pltpu.VMEM),
        scratch_shapes=[
            pltpu.VMEM((BLOCKS, 16, half), f32),
            pltpu.VMEM((16, targets), f32),
            pltpu.VMEM((3, 16, targets), f32),
            pltpu.VMEM((3, 96, targets), bf16),
            pltpu.VMEM((2, 3, CHUNK * half, targets), f32),
            pltpu.VMEM((3, 48, targets), f32),
            pltpu.VMEM((3, 32, targets), f32),
            pltpu.VMEM((16, targets), f32),
            pltpu.VMEM((16, targets), f32),
            pltpu.SemaphoreType.DMA((count,)),
            pltpu.SemaphoreType.DMA((count,)),
            pltpu.SemaphoreType.DMA((2,)),
        ],
        compiler_params=pltpu.CompilerParams(
            collective_id=0, has_side_effects=True, vmem_limit_bytes=48 * 2**20
        ),
    )(positions, velocities, accelerations, jerks, snaps, masses.reshape(1, targets))
    return correct(positions, velocities, accelerations, jerks, snaps, forces)


def solution(mesh):
    return jax.shard_map(
        shards,
        mesh=mesh,
        in_specs=(P(None, "wide"),) * 5 + (P("wide"),),
        out_specs=(P(None, "wide"),) * 6,
        check_vma=False,
    )
```

time: 768 us -> 91 us (0.12); the launches traced: 757 us -> 90.6 us
  other arithmetic: 467 us -> 1.23 us
  waiting for transfers between devices: 124 us -> 0 us
  local copies, waits for them, and re-layouts: 124 us -> 4.17 us
  Pallas kernels: 0 us -> 84.5 us
  blocking collectives: 26 us -> 0 us
  between operations: 14.1 us -> 0.66 us
    reduce_sum x128 -> x0, other arithmetic: 330 us -> none  [the longest x64 172 us: pair_forces(): dist_sq = jnp.sum(separation * separation, axis=0) + softening]
    mul x64 -> x0, other arithmetic: 134 us -> none  [pair_forces(): 6.0 * radial * jerk_pair]
    all_gather x1 -> x0, waiting for transfers between devices: 124 us -> none  [shards(): lax.all_gather(source, 'wide', axis=1, tiled=True)]
    pallas_call x0 -> x1, Pallas kernels: none -> 84.5 us  [shards(): pl.pallas_call(forces_kernel, out_shape=jax.ShapeDtypeStruct((16, targets...]
    sub x64 -> x0, local copies, waits for them, and re-layouts: 62.4 us -> none  [pair_forces(): relative_vel = sources[3:6, None, :] - targets[3:6, :, None]]
    slice x128 -> x0, local copies, waits for them, and re-layouts: 49.2 us -> none  [the longest x64 48.9 us: pair_forces(): strength = sources[9][None, :] * inverse_sq * jnp.sqrt(inverse_sq)]
    all_gather x6 -> x0, blocking collectives: 26 us -> none  [the longest x1 4.34 us: shards(): lax.all_gather(new_pos, 'narrow', axis=1, tiled=True)]
  transfers between devices with their start and end apart: 1 -> 0, of which waited for: 1 -> 0; matrix products, arithmetic and copies ran while one was open for 0% -> 0% of each run, Pallas kernels for 0% -> 0%
where the time goes in v1:
time: 91 us; the launch traced here: 90.6 us
  Pallas kernels  84.5 us (93%)
  local copies, waits for them, and re-layouts  4.17 us (5%)
  other arithmetic  1.23 us (1%)
    pallas_call x1, Pallas kernels, shards(): pl.pallas_call(forces_kernel, out_shape=jax.ShapeDtypeStruct((16, targets...  84.5 us
    unnamed x18, local copies, waits for them, and re-layouts  4.17 us

profile of v1, /device:TPU:2, one launch (start us, length us, event | category | flops | bytes accessed | tf_op | source)
XLA Modules:
  0.0 90.6 jit_solution(7775898914022025939)
XLA Ops:
  0.6 0.0 copy-start
  0.6 0.7 copy-done
  1.3 0.0 copy-start.1
  1.3 0.7 copy-done.1
  2.0 0.0 copy-start.2
  2.0 0.7 copy-done.2
  2.7 0.0 copy-start.3
  2.7 0.7 copy-done.3
  3.4 0.0 copy-start.4
  3.4 0.7 copy-done.4
  4.1 0.0 copy-start.5
  4.1 0.7 copy-done.5
  4.8 84.5 %shard_map.109 = f32[16,512]{1,0:T(8,128)S(1)} custom-call(f32[3,512]{1,0:T(4,128)S(1)} %copy-done.3, f32[3,512]{1,0:T(4,128)S(1)} %copy-done.4, f32[3,512]{1,0:T(4,128)S(1)} %copy-done.2, f32[3,512]{1,0:T(4,128)S(1)} %copy-done.1, f32[3,512]{1,0:T(4,128)S(1)} %copy-done, f32[1,512]{1,0:T(1,128)S(1)} %bitcast.1), custom_call_target="tpu_custom_call" | custom-call | tf_op jit(solution)/shard_map/pallas_call | solution.py:353
  89.3 0.6 multiply_add_fusion
  90.0 0.0 copy-start.6
  90.0 0.0 copy-start.7
  90.0 0.0 copy-start.8
  90.0 0.6 multiply_add_fusion.1
  90.6 0.0 copy-done.6
  90.6 0.0 copy-done.7
  90.6 0.0 copy-done.8
Async XLA Ops:
  0.6 0.7 copy-start
  1.3 0.7 copy-start.1
  2.0 0.7 copy-start.2
  2.7 0.7 copy-start.3
  3.4 0.7 copy-start.4
  4.1 0.7 copy-start.5
  90.0 0.6 copy-start.6
  90.0 0.6 copy-start.7
  90.0 0.6 copy-start.8

commit v2 on v1

--- a/solution.py
+++ b/solution.py
@@ -13,6 +13,7 @@
 bf16 = jnp.bfloat16
 f32 = jnp.float32
 f8 = jnp.float8_e4m3fn
+f8_wide = jnp.float8_e5m2
 MESH = pl.DeviceIdType.MESH
 
 CORES, NZ, NX, NY = 2, 8, 2, 4
@@ -23,11 +24,12 @@
 TILE = 256
 
 Q_SCALE = 2.0**-4
-P_SCALE = 2.0**-10.5
-G_SCALE = 0.2 * 2.0**-17
+P_SCALE = 2.0**-9.5
+G_SCALE = 0.2 * 2.0**-15
 W_BACK = 2.0**-6
-C1_BACK = 2.0**0.5
-C2_BACK = 2.0**7
+C1_BACK = 2.0**-0.5
+C2_BACK = 2.0**5
+FINE_ROWS = ((0, 32), (32, 64), (64, 80))
 
 
 def predict(positions, velocities, accelerations, jerks, snaps):
@@ -77,47 +79,34 @@
     def put(step, to, src, dst, count=1):
         plan.append((step, to, src, dst, count))
 
-    for to, dst in (("core", 1), ("z+", 2), ("z-", 3), ("y+", 4), ("y-", 5), ("x", 17)):
+    for to, dst in (
+        ("core", 1), ("y+", 2), ("y-", 3), ("x", 4), ("y+ core", 5), ("z-", 16), ("z+", 32),
+    ):
         put(-1, to, 0, dst)
-    put(0, "z+", 2, 8)
-    put(0, "z-", 3, 9)
-    put(0, "core", 2, 6, 2)
-    put(0, "y+", 2, 19, 2)
-    put(0, "y-", 2, 34, 2)
-    put(0, "x", 2, 65, 2)
-    put(0, "core", 4, 26)
-    put(0, "core", 5, 41)
-    put(0, "y+", 4, 49)
-    put(0, "x", 4, 80)
-    put(0, "x", 5, 96)
-    put(1, "z+", 8, 12)
-    put(1, "z-", 9, 13)
+    put(0, "y+", 2, 12)
+    put(0, "x", 2, 8, 2)
+    put(0, "core", 3, 6, 2)
+    put(0, "z-", 2, 17, 3)
+    put(0, "z+", 2, 33, 3)
+    put(1, "x", 12, 13)
     put(1, "core", 8, 10, 2)
-    put(1, "y+", 8, 21, 2)
-    put(1, "y-", 8, 36, 2)
-    put(1, "x", 8, 67, 2)
-    put(2, "z+", 12, 16)
+    put(1, "z-", 8, 20, 2)
+    put(1, "z+", 8, 36, 2)
     put(2, "core", 12, 14, 2)
-    put(2, "y+", 12, 23, 2)
-    put(2, "y-", 12, 38, 2)
-    put(2, "x", 12, 69, 2)
-    put(3, "core", 16, 18)
-    put(3, "y+", 16, 25)
-    put(3, "y-", 16, 40)
-    put(3, "x", 16, 71)
-    put(3, "core", 17, 72)
-    put(4, "y+", 19, 50, 3)
-    put(5, "core", 19, 27, 7)
-    put(5, "x", 19, 81, 7)
-    put(5, "y-", 37, 53, 4)
-    put(5, "core", 34, 42, 7)
-    put(5, "x", 34, 97, 7)
-    put(8, "core", 49, 57, 8)
-    put(8, "x", 49, 112, 8)
-    put(12, "core", 65, 73, 7)
-    put(14, "core", 80, 88, 8)
-    put(16, "core", 96, 104, 8)
-    put(18, "core", 112, 120, 8)
+    put(2, "z-", 12, 22, 2)
+    put(2, "z+", 12, 38, 2)
+    put(4, "core", 16, 24, 8)
+    put(4, "z-", 16, 48, 8)
+    put(7, "core", 32, 40, 8)
+    put(7, "z+", 32, 64, 8)
+    put(8, "core", 48, 56, 8)
+    put(8, "z-", 48, 80, 8)
+    put(11, "core", 64, 72, 8)
+    put(11, "z+", 64, 96, 8)
+    put(12, "core", 80, 88, 8)
+    put(12, "z-", 80, 112, 8)
+    put(15, "core", 96, 104, 8)
+    put(16, "core", 112, 120, 8)
     return plan
 
 
@@ -152,19 +141,38 @@
 
 
 def sum_rows(block):
-    weighed = block * block[12:13]
-    fine = jnp.concatenate(split3(weighed), axis=0)
-    high = weighed.astype(f8)
-    rest = (weighed - high.astype(f32)).astype(f8)
-    coarse = jnp.concatenate([high.astype(f32), rest.astype(f32)], axis=0).astype(f8)
-    return fine, coarse
+    weighed = block * block[7:8]
+    high, middle, low = [part.astype(f32) for part in split3(weighed)]
+    none = jnp.zeros_like(weighed[0:8])
+    fine = (
+        jnp.concatenate([high, middle], axis=0).astype(bf16),
+        jnp.concatenate([high[0:8], middle[0:8], low[0:8], none], axis=0).astype(bf16),
+        jnp.concatenate([high[0:4], middle[0:4], low[0:4], none[0:4]], axis=0).astype(bf16),
+    )
+    first = weighed.astype(f8).astype(f32)
+    second = weighed - first
+    narrow = jnp.concatenate([first, second], axis=0).astype(f8)
+    first = weighed[0:8].astype(f8_wide).astype(f32)
+    second = (weighed[0:8] - first).astype(f8_wide).astype(f32)
+    third = weighed[0:8] - first - second
+    broad = jnp.concatenate([first, second, third, none], axis=0).astype(f8_wide)
+    return fine, (narrow, narrow, broad)
 
 
 def forces_kernel(
-    pos_ref, vel_ref, acc_ref, jerk_ref, snap_ref, mass_ref, out_ref,
-    slots, own, feature, weights, pairs, total, total_low, part, other,
-    send_sem, recv_sem, narrow_sem,
+    pos_hbm, vel_hbm, acc_hbm, jerk_hbm, snap_hbm, mass_hbm, out_ref,
+    pos_ref, vel_ref, acc_ref, jerk_ref, snap_ref, mass_ref, slots, own, feature, weights, pairs, total, total_low, part, other,
+    load_sem, send_sem, recv_sem, narrow_sem,
 ):
+    loads = [
+        pltpu.make_async_copy(src, dst, load_sem.at[number])
+        for number, (src, dst) in enumerate((
+            (pos_hbm, pos_ref), (vel_hbm, vel_ref), (acc_hbm, acc_ref),
+            (jerk_hbm, jerk_ref), (snap_hbm, snap_ref), (mass_hbm, mass_ref),
+        ))
+    ]
+    for load in loads:
+        load.start()
     wide, narrow = lax.axis_index("wide"), lax.axis_index("narrow")
     core, z = wide % CORES, (wide // CORES) % NZ
     x, y = (wide // (CORES * NZ)) % NX, wide // (CORES * NZ * NX)
@@ -179,11 +187,16 @@
         "y+": {"wide": index((y + 1) % NY, x, z, core)},
         "y-": {"wide": index((y + NY - 1) % NY, x, z, core)},
         "x": {"wide": index(y, 1 - x, z, core)},
+        "y+ core": {"wide": index((y + 1) % NY, x, z, 1 - core)},
         "narrow": {"narrow": 1 - narrow},
     }
     barrier = pltpu.get_barrier_semaphore()
-    for device in partner.values():
+    senders = dict(partner)
+    senders["y+ core"] = {"wide": index((y + NY - 1) % NY, x, z, 1 - core)}
+    for device in senders.values():
         pl.semaphore_signal(barrier, inc=1, device_id=device, device_id_type=MESH)
+    for load in loads:
+        load.wait()
 
     star_x, star_v, star_a = predict(
         pos_ref[...], vel_ref[...], acc_ref[...], jerk_ref[...], snap_ref[...]
@@ -198,8 +211,7 @@
     one = jnp.ones_like(xx)
     own[...] = jnp.zeros_like(own)
     for row, value in (
-        (0, star_x), (3, star_v), (6, star_a), (9, xx), (10, xv), (11, vv),
-        (12, mass_ref[...]), (13, one),
+        (0, star_x), (3, one), (4, star_v), (7, mass_ref[...]), (8, star_a), (11, xx), (12, xv), (13, vv),
     ):
         own[row : row + value.shape[0], :] = value
     start = pl.multiple_of(narrow * half, half)
@@ -237,11 +249,11 @@
 
     feature[...] = jnp.zeros_like(feature)
     for kind, rows in enumerate((
-        ((0, -2.0 * Q_SCALE * star_x), (9, Q_SCALE * one), (13, Q_SCALE * (xx + softening))),
-        ((0, -P_SCALE * star_v), (3, -P_SCALE * star_x), (10, P_SCALE * one), (13, P_SCALE * xv)),
+        ((0, -2.0 * Q_SCALE * star_x), (3, Q_SCALE * (xx + softening)), (11, Q_SCALE * one)),
+        ((0, -P_SCALE * star_v), (3, P_SCALE * xv), (4, -P_SCALE * star_x), (12, P_SCALE * one)),
         (
-            (0, -G_SCALE * star_a), (3, -2.0 * G_SCALE * star_v), (6, -G_SCALE * star_x),
-            (11, G_SCALE * one), (13, G_SCALE * vv),
+            (0, -G_SCALE * star_a), (3, G_SCALE * vv), (4, -2.0 * G_SCALE * star_v),
+            (8, -G_SCALE * star_x), (13, G_SCALE * one),
         ),
     )):
         for row, value in rows:
@@ -302,9 +314,10 @@
                 c2 = (w * inverse) * (p * radial - g)
                 for kind, value in enumerate((w, c1, c2)):
                     high = value.astype(bf16)
-                    low = (value - high.astype(f32)).astype(f8)
-                    total[kind, :, columns] += product(fine[:, js], high, 1)
-                    total_low[kind, :, columns] += product(coarse[:, js], low, 1)
+                    low = (value - high.astype(f32)).astype(coarse[kind].dtype)
+                    begin, end = FINE_ROWS[kind]
+                    total[begin:end, columns] += product(fine[kind][:, js], high, 1)
+                    total_low[kind, :, columns] += product(coarse[kind][:, js], low, 1)
                 until = (place + 1) * len(work) // len(units)
                 for kind, at in work[done:until]:
                     forward(ahead, later, kind, at)
@@ -313,23 +326,22 @@
 
     lax.fori_loop(0, steps, body, 0)
 
-    sums = []
-    for kind in range(3):
-        sums.append(
-            total[kind, 0:16] + total[kind, 16:32] + total[kind, 32:48]
-            + total_low[kind, 0:16] + total_low[kind, 16:32]
-        )
-    sw, s1, s2 = sums
+    sw = total[0:16] + total[16:32] + total_low[0, 0:16] + total_low[0, 16:32]
+    s1 = total[32:40] + total[40:48] + total[48:56] + total_low[1, 0:8] + total_low[1, 16:24]
+    s2 = (
+        total[64:68] + total[68:72] + total[72:76]
+        + total_low[2, 0:4] + total_low[2, 8:12] + total_low[2, 16:20]
+    )
     share = 1.0 / (targets * BLOCKS)
-    star_x, star_v, star_a = own[0:3, :], own[3:6, :], own[6:9, :]
+    star_x, star_v, star_a = own[0:3, :], own[4:7, :], own[8:11, :]
     part[...] = jnp.zeros_like(part)
-    part[0:3, :] = (W_BACK * share) * (sw[0:3] - star_x * sw[13:14])
-    c1x = (C1_BACK * share) * (s1[0:3] - star_x * s1[13:14])
-    part[3:6, :] = (W_BACK * share) * (sw[3:6] - star_v * sw[13:14]) - 3.0 * c1x
+    part[0:3, :] = (W_BACK * share) * (sw[0:3] - star_x * sw[3:4])
+    c1x = (C1_BACK * share) * (s1[0:3] - star_x * s1[3:4])
+    part[3:6, :] = (W_BACK * share) * (sw[4:7] - star_v * sw[3:4]) - 3.0 * c1x
     part[6:9, :] = (
-        (W_BACK * share) * (sw[6:9] - star_a * sw[13:14])
-        - (6.0 * C1_BACK * share) * (s1[3:6] - star_v * s1[13:14])
-        + (15.0 * C2_BACK * share) * (s2[0:3] - star_x * s2[13:14])
+        (W_BACK * share) * (sw[8:11] - star_a * sw[3:4])
+        - (6.0 * C1_BACK * share) * (s1[4:7] - star_v * s1[3:4])
+        + (15.0 * C2_BACK * share) * (s2[0:3] - star_x * s2[3:4])
     )
     swap = pltpu.make_async_remote_copy(
         src_ref=part,
@@ -353,24 +365,27 @@
     forces = pl.pallas_call(
         forces_kernel,
         out_shape=jax.ShapeDtypeStruct((16, targets), f32),
-        in_specs=[pl.BlockSpec(memory_space=pltpu.VMEM)] * 6,
+        in_specs=[pl.BlockSpec(memory_space=pltpu.HBM)] * 6,
         out_specs=pl.BlockSpec(memory_space=pltpu.VMEM),
-        scratch_shapes=[
+        scratch_shapes=[pltpu.VMEM((3, targets), f32) for _ in range(5)]
+        + [
+            pltpu.VMEM((1, targets), f32),
             pltpu.VMEM((BLOCKS, 16, half), f32),
             pltpu.VMEM((16, targets), f32),
             pltpu.VMEM((3, 16, targets), f32),
             pltpu.VMEM((3, 96, targets), bf16),
             pltpu.VMEM((2, 3, CHUNK * half, targets), f32),
-            pltpu.VMEM((3, 48, targets), f32),
+            pltpu.VMEM((80, targets), f32),
             pltpu.VMEM((3, 32, targets), f32),
             pltpu.VMEM((16, targets), f32),
             pltpu.VMEM((16, targets), f32),
+            pltpu.SemaphoreType.DMA((6,)),
             pltpu.SemaphoreType.DMA((count,)),
             pltpu.SemaphoreType.DMA((count,)),
             pltpu.SemaphoreType.DMA((2,)),
         ],
         compiler_params=pltpu.CompilerParams(
-            collective_id=0, has_side_effects=True, vmem_limit_bytes=48 * 2**20
+            collective_id=0, has_side_effects=True, vmem_limit_bytes=60 * 2**20
         ),
     )(positions, velocities, accelerations, jerks, snaps, masses.reshape(1, targets))
     return correct(positions, velocities, accelerations, jerks, snaps, forces)

time: 91 us -> 86.8 us (0.954)
  local copies, waits for them, and re-layouts: 4.17 us -> 0.04 us
  Pallas kernels: 84.5 us -> 83.3 us
    unnamed x18 -> x16, local copies, waits for them, and re-layouts: 4.17 us -> 0.04 us
    pallas_call x1, Pallas kernels: 84.5 us -> 83.3 us  [shards(): pl.pallas_call(forces_kernel, out_shape=jax.ShapeDtypeStruct((16, targets...]
where the time goes in v2:
time: 86.8 us; the launch traced here: 86.1 us
  Pallas kernels  83.3 us (96%)
  other arithmetic  2.1 us (2%)
    pallas_call x1, Pallas kernels, shards(): pl.pallas_call(forces_kernel, out_shape=jax.ShapeDtypeStruct((16, targets...  83.3 us

profile of v2, /device:TPU:2, one launch (start us, length us, event | category | flops | bytes accessed | tf_op | source)
XLA Modules:
  0.0 86.1 jit_solution(8400751362714963599)
XLA Ops:
  0.6 0.0 copy-start
  0.6 0.0 copy-start.1
  0.7 0.0 copy-start.2
  0.7 83.3 %shard_map.109 = f32[16,512]{1,0:T(8,128)} custom-call(f32[3,512]{1,0:T(4,128)} %pos_hbm.1, f32[3,512]{1,0:T(4,128)} %vel_hbm.1, f32[3,512]{1,0:T(4,128)} %acc_hbm.1, f32[3,512]{1,0:T(4,128)} %jerk_hbm.1, f32[3,512]{1,0:T(4,128)} %snap_hbm.1, f32[1,512]{1,0:T(1,128)} %bitcast.1), custom_call_target="tpu_custom_call" | custom-call | tf_op jit(solution)/shard_map/pallas_call | solution.py:365
  83.9 0.0 copy-done
  84.0 0.0 copy-done.1
  84.0 0.0 copy-done.2
  84.0 0.0 copy-start.3
  84.0 0.0 copy-start.4
  84.0 1.5 %multiply_add_fusion = (f32[3,512]{1,0:T(4,128)}, f32[3,512]{1,0:T(4,128)S(1)}, f32[3,512]{1,0:T(4,128)S(1)}, f32[3,512]{1,0:T(4,128)S(1)}) fusion(f32[3,512]{1,0:T(4,128)S(1)} %copy-done, f32[3,512]{1,0:T(4,128)S(1)} %copy-done.1, f32[3,512]{1,0:T(4,128)S(1)} %copy-done.2, f32[16,512]{1,0:T(8,128)} %shard_map.109), kind=kLoop, calls=%fused_computation | loop fusion | flops 21504 | bytes 61440 | tf_op jit(solution)/shard_map/add | solution.py:72
  85.5 0.0 copy-start.5
  85.5 0.0 copy-start.6
  85.5 0.0 copy-start.7
  85.5 0.0 copy-done.3
  85.5 0.0 copy-done.4
  85.5 0.6 multiply_add_fusion.1
  86.1 0.0 copy-done.5
  86.1 0.0 copy-done.6
  86.1 0.0 copy-done.7
Async XLA Ops:
  0.6 83.3 %copy-start = (f32[3,512]{1,0:T(4,128)S(1)}, f32[3,512]{1,0:T(4,128)}, u32[]{:S(2)}) copy-start(f32[3,512]{1,0:T(4,128)} %snap_hbm.1) | copy-start | bytes 18436
  0.6 83.3 %copy-start.1 = (f32[3,512]{1,0:T(4,128)S(1)}, f32[3,512]{1,0:T(4,128)}, u32[]{:S(2)}) copy-start(f32[3,512]{1,0:T(4,128)} %jerk_hbm.1) | copy-start | bytes 18436
  0.7 83.3 %copy-start.2 = (f32[3,512]{1,0:T(4,128)S(1)}, f32[3,512]{1,0:T(4,128)}, u32[]{:S(2)}) copy-start(f32[3,512]{1,0:T(4,128)} %acc_hbm.1) | copy-start | bytes 18436
  84.0 1.5 %copy-start.3 = (f32[3,512]{1,0:T(4,128)S(1)}, f32[3,512]{1,0:T(4,128)}, u32[]{:S(2)}) copy-start(f32[3,512]{1,0:T(4,128)} %pos_hbm.1) | copy-start | bytes 18436
  84.0 1.5 %copy-start.4 = (f32[3,512]{1,0:T(4,128)S(1)}, f32[3,512]{1,0:T(4,128)}, u32[]{:S(2)}) copy-start(f32[3,512]{1,0:T(4,128)} %vel_hbm.1) | copy-start | bytes 18436
  85.5 0.6 copy-start.5
  85.5 0.6 copy-start.6
  85.5 0.6 copy-start.7

commit v3 on v2

--- a/solution.py
+++ b/solution.py
@@ -21,6 +21,8 @@
 CHUNK = 2
 PARTS = 2
 STEP = CHUNK * PARTS
+EARLY = 8
+LATE_PARTS = 4
 TILE = 256
 
 Q_SCALE = 2.0**-4
@@ -79,33 +81,30 @@
     def put(step, to, src, dst, count=1):
         plan.append((step, to, src, dst, count))
 
-    for to, dst in (
-        ("core", 1), ("y+", 2), ("y-", 3), ("x", 4), ("y+ core", 5), ("z-", 16), ("z+", 32),
-    ):
+    for to, dst in (("core", 1), ("y+", 2), ("y-", 3), ("x", 4), ("y+ core", 5)):
         put(-1, to, 0, dst)
     put(0, "y+", 2, 12)
     put(0, "x", 2, 8, 2)
     put(0, "core", 3, 6, 2)
-    put(0, "z-", 2, 17, 3)
-    put(0, "z+", 2, 33, 3)
     put(1, "x", 12, 13)
     put(1, "core", 8, 10, 2)
-    put(1, "z-", 8, 20, 2)
-    put(1, "z+", 8, 36, 2)
+    for first, to, base in ((2, "z-", 16), (1, "z+", 32)):
+        put(first, to, 0, base)
+        put(first, to, 2, base + 1, 3)
+        put(first, to, 8, base + 4, 2)
+        put(2, to, 12, base + 6, 2)
     put(2, "core", 12, 14, 2)
-    put(2, "z-", 12, 22, 2)
-    put(2, "z+", 12, 38, 2)
     put(4, "core", 16, 24, 8)
     put(4, "z-", 16, 48, 8)
     put(7, "core", 32, 40, 8)
     put(7, "z+", 32, 64, 8)
     put(8, "core", 48, 56, 8)
     put(8, "z-", 48, 80, 8)
-    put(11, "core", 64, 72, 8)
-    put(11, "z+", 64, 96, 8)
+    put(12, "core", 64, 72, 8)
+    put(12, "z+", 64, 96, 8)
     put(12, "core", 80, 88, 8)
     put(12, "z-", 80, 112, 8)
-    put(15, "core", 96, 104, 8)
+    put(16, "core", 96, 104, 8)
     put(16, "core", 112, 120, 8)
     return plan
 
@@ -114,6 +113,8 @@
     due = []
     for _, _, _, dst, count in plan:
         use = max(-1, -((5 - dst) // STEP))
+        if use >= EARLY:
+            use -= (use - EARLY) % (LATE_PARTS // PARTS)
         for step, _, src, _, length in plan:
             if src < dst + count and dst < src + length:
                 use = min(use, step)
@@ -162,7 +163,7 @@
 def forces_kernel(
     pos_hbm, vel_hbm, acc_hbm, jerk_hbm, snap_hbm, mass_hbm, out_ref,
     pos_ref, vel_ref, acc_ref, jerk_ref, snap_ref, mass_ref, slots, own, feature, weights, pairs, total, total_low, part, other,
-    load_sem, send_sem, recv_sem, narrow_sem,
+    far_sem, load_sem, send_sem, recv_sem, narrow_sem,
 ):
     loads = [
         pltpu.make_async_copy(src, dst, load_sem.at[number])
@@ -193,8 +194,9 @@
     barrier = pltpu.get_barrier_semaphore()
     senders = dict(partner)
     senders["y+ core"] = {"wide": index((y + NY - 1) % NY, x, z, 1 - core)}
-    for device in senders.values():
-        pl.semaphore_signal(barrier, inc=1, device_id=device, device_id_type=MESH)
+    for to, device in senders.items():
+        if to != "z+":
+            pl.semaphore_signal(barrier, inc=1, device_id=device, device_id_type=MESH)
     for load in loads:
         load.wait()
 
@@ -216,7 +218,8 @@
         own[row : row + value.shape[0], :] = value
     start = pl.multiple_of(narrow * half, half)
     slots[0] = own[:, pl.ds(start, half)]
-    pl.semaphore_wait(barrier, len(partner))
+    pl.semaphore_wait(barrier, len(partner) - 1)
+    pl.semaphore_signal(far_sem, inc=1, device_id=partner["z+"], device_id_type=MESH)
 
     plan = transfers()
     due = waits(plan)
@@ -236,6 +239,8 @@
         for number in range(len(plan)):
             if due[number] == step and plan[number][0] < step:
                 copy(number).wait_recv()
+        if step == min(t[0] for t in plan if t[1] == "z-"):
+            pl.semaphore_wait(far_sem, 1)
         for number in range(len(plan)):
             if plan[number][0] == step:
                 copy(number).start()
@@ -279,7 +284,6 @@
         for tile in range(targets // TILE):
             forward(rows, 0, kind, tile)
 
-    steps = BLOCKS // STEP
     events = sorted(set([d for d in due if d >= 0] + [t[0] for t in plan if t[0] >= 0]))
 
     def branch(step, numbers):
@@ -292,22 +296,22 @@
         pl.when(step < second[0])(functools.partial(branch, step, first))
         pl.when(step >= second[0])(functools.partial(branch, step, second))
 
-    def body(step, carry):
-        branch(step, events)
-        for parity in range(PARTS):
+    def body(parts, numbers, step, carry):
+        branch(step, numbers)
+        for parity in range(parts):
             chunk = step * PARTS + parity
             now, later = parity % 2, (parity + 1) % 2
             fine, coarse = sum_rows(chunk_of(chunk))
             ahead = source_rows(chunk_of(lax.min(chunk + 1, BLOCKS // CHUNK - 1)))
-            work = [(kind, tile) for kind in range(3) for tile in range(targets // TILE)]
-            units = [(b, tile) for b in range(CHUNK) for tile in range(targets // TILE)]
+            work = [(kind, tile) for tile in range(targets // TILE) for kind in range(3)]
+            units = [(b, tile) for tile in range(targets // TILE) for b in range(CHUNK)]
             done = 0
             for place, (b, tile) in enumerate(units):
                 js = slice(b * half, (b + 1) * half)
                 columns = slice(tile * TILE, (tile + 1) * TILE)
                 q, p, g = [pairs[now, kind, js, columns] for kind in range(3)]
                 root = lax.rsqrt(q)
-                inverse = root * root
+                inverse = pl.reciprocal(q, approx=True)
                 w = inverse * root
                 radial = p * inverse
                 c1 = radial * w
@@ -324,7 +328,12 @@
                 done = until
         return carry
 
-    lax.fori_loop(0, steps, body, 0)
+    early = functools.partial(body, PARTS, [e for e in events if e < EARLY])
+    lax.fori_loop(0, EARLY, early, 0)
+    late = functools.partial(body, LATE_PARTS, [e for e in events if e >= EARLY])
+    stride = LATE_PARTS // PARTS
+    steps = (BLOCKS // STEP - EARLY) // stride
+    lax.fori_loop(0, steps, lambda number, carry: late(EARLY + stride * number, carry), 0)
 
     sw = total[0:16] + total[16:32] + total_low[0, 0:16] + total_low[0, 16:32]
     s1 = total[32:40] + total[40:48] + total[48:56] + total_low[1, 0:8] + total_low[1, 16:24]
@@ -379,6 +388,7 @@
             pltpu.VMEM((3, 32, targets), f32),
             pltpu.VMEM((16, targets), f32),
             pltpu.VMEM((16, targets), f32),
+            pltpu.SemaphoreType.REGULAR,
             pltpu.SemaphoreType.DMA((6,)),
             pltpu.SemaphoreType.DMA((count,)),
             pltpu.SemaphoreType.DMA((count,)),

time: 86.8 us -> 82.1 us (0.946)
  Pallas kernels: 83.3 us -> 77.7 us
    pallas_call x1, Pallas kernels: 83.3 us -> 77.7 us  [shards(): pl.pallas_call(forces_kernel, out_shape=jax.ShapeDtypeStruct((16, targets...]
where the time goes in v3:
time: 82.1 us; the launch traced here: 80.6 us
  Pallas kernels  77.7 us (95%)
  other arithmetic  2.11 us (3%)
    pallas_call x1, Pallas kernels, shards(): pl.pallas_call(forces_kernel, out_shape=jax.ShapeDtypeStruct((16, targets...  77.7 us

profile of v3, /device:TPU:2, one launch (start us, length us, event | category | flops | bytes accessed | tf_op | source)
XLA Modules:
  0.0 80.6 jit_solution(132820142791659716)
XLA Ops:
  0.6 0.0 copy-start
  0.6 0.0 copy-start.1
  0.7 0.0 copy-start.2
  0.7 77.7 %shard_map.109 = f32[16,512]{1,0:T(8,128)} custom-call(f32[3,512]{1,0:T(4,128)} %pos_hbm.1, f32[3,512]{1,0:T(4,128)} %vel_hbm.1, f32[3,512]{1,0:T(4,128)} %acc_hbm.1, f32[3,512]{1,0:T(4,128)} %jerk_hbm.1, f32[3,512]{1,0:T(4,128)} %snap_hbm.1, f32[1,512]{1,0:T(1,128)} %bitcast.1), custom_call_target="tpu_custom_call" | custom-call | tf_op jit(solution)/shard_map/pallas_call | solution.py:374
  78.4 0.0 copy-done
  78.4 0.0 copy-done.1
  78.4 0.0 copy-done.2
  78.4 0.0 copy-start.3
  78.4 0.0 copy-start.4
  78.5 1.5 %multiply_add_fusion = (f32[3,512]{1,0:T(4,128)}, f32[3,512]{1,0:T(4,128)S(1)}, f32[3,512]{1,0:T(4,128)S(1)}, f32[3,512]{1,0:T(4,128)S(1)}) fusion(f32[3,512]{1,0:T(4,128)S(1)} %copy-done, f32[3,512]{1,0:T(4,128)S(1)} %copy-done.1, f32[3,512]{1,0:T(4,128)S(1)} %copy-done.2, f32[16,512]{1,0:T(8,128)} %shard_map.109), kind=kLoop, calls=%fused_computation | loop fusion | flops 21504 | bytes 61440 | tf_op jit(solution)/shard_map/add | solution.py:74
  79.9 0.0 copy-start.5
  79.9 0.0 copy-start.6
  79.9 0.0 copy-start.7
  79.9 0.0 copy-done.3
  80.0 0.0 copy-done.4
  80.0 0.6 multiply_add_fusion.1
  80.6 0.0 copy-done.5
  80.6 0.0 copy-done.6
  80.6 0.0 copy-done.7
Async XLA Ops:
  0.6 77.8 %copy-start = (f32[3,512]{1,0:T(4,128)S(1)}, f32[3,512]{1,0:T(4,128)}, u32[]{:S(2)}) copy-start(f32[3,512]{1,0:T(4,128)} %snap_hbm.1) | copy-start | bytes 18436
  0.6 77.8 %copy-start.1 = (f32[3,512]{1,0:T(4,128)S(1)}, f32[3,512]{1,0:T(4,128)}, u32[]{:S(2)}) copy-start(f32[3,512]{1,0:T(4,128)} %jerk_hbm.1) | copy-start | bytes 18436
  0.7 77.8 %copy-start.2 = (f32[3,512]{1,0:T(4,128)S(1)}, f32[3,512]{1,0:T(4,128)}, u32[]{:S(2)}) copy-start(f32[3,512]{1,0:T(4,128)} %acc_hbm.1) | copy-start | bytes 18436
  78.4 1.5 %copy-start.3 = (f32[3,512]{1,0:T(4,128)S(1)}, f32[3,512]{1,0:T(4,128)}, u32[]{:S(2)}) copy-start(f32[3,512]{1,0:T(4,128)} %pos_hbm.1) | copy-start | bytes 18436
  78.4 1.5 %copy-start.4 = (f32[3,512]{1,0:T(4,128)S(1)}, f32[3,512]{1,0:T(4,128)}, u32[]{:S(2)}) copy-start(f32[3,512]{1,0:T(4,128)} %vel_hbm.1) | copy-start | bytes 18436
  79.9 0.6 copy-start.5
  79.9 0.6 copy-start.6
  79.9 0.6 copy-start.7

commit v4 on v3

--- a/solution.py
+++ b/solution.py
@@ -22,7 +22,8 @@
 PARTS = 2
 STEP = CHUNK * PARTS
 EARLY = 8
-LATE_PARTS = 4
+LATE_PARTS = 8
+FIRST_Z = 1
 TILE = 256
 
 Q_SCALE = 2.0**-4
@@ -88,11 +89,11 @@
     put(0, "core", 3, 6, 2)
     put(1, "x", 12, 13)
     put(1, "core", 8, 10, 2)
-    for first, to, base in ((2, "z-", 16), (1, "z+", 32)):
-        put(first, to, 0, base)
-        put(first, to, 2, base + 1, 3)
-        put(first, to, 8, base + 4, 2)
-        put(2, to, 12, base + 6, 2)
+    for to, base in (("z-", 16), ("z+", 32)):
+        put(FIRST_Z, to, 0, base)
+        put(FIRST_Z, to, 2, base + 1, 3)
+        put(FIRST_Z, to, 8, base + 4, 2)
+        put(FIRST_Z + 1, to, 12, base + 6, 2)
     put(2, "core", 12, 14, 2)
     put(4, "core", 16, 24, 8)
     put(4, "z-", 16, 48, 8)
@@ -194,9 +195,18 @@
     barrier = pltpu.get_barrier_semaphore()
     senders = dict(partner)
     senders["y+ core"] = {"wide": index((y + NY - 1) % NY, x, z, 1 - core)}
+    lowest, highest = z == 0, z == NZ - 1
     for to, device in senders.items():
-        if to != "z+":
+        if to not in ("z+", "z-"):
             pl.semaphore_signal(barrier, inc=1, device_id=device, device_id_type=MESH)
+
+    @pl.when(jnp.logical_not(highest))
+    def _():
+        pl.semaphore_signal(barrier, inc=1, device_id=partner["z+"], device_id_type=MESH)
+
+    @pl.when(lowest)
+    def _():
+        pl.semaphore_signal(barrier, inc=1, device_id=partner["z-"], device_id_type=MESH)
     for load in loads:
         load.wait()
 
@@ -218,8 +228,15 @@
         own[row : row + value.shape[0], :] = value
     start = pl.multiple_of(narrow * half, half)
     slots[0] = own[:, pl.ds(start, half)]
-    pl.semaphore_wait(barrier, len(partner) - 1)
-    pl.semaphore_signal(far_sem, inc=1, device_id=partner["z+"], device_id_type=MESH)
+    pl.semaphore_wait(barrier, len(partner) - 2 + lax.min(z, 1) + z // (NZ - 1))
+
+    @pl.when(jnp.logical_not(lowest))
+    def _():
+        pl.semaphore_signal(far_sem.at[0], inc=1, device_id=partner["z-"], device_id_type=MESH)
+
+    @pl.when(highest)
+    def _():
+        pl.semaphore_signal(far_sem.at[1], inc=1, device_id=partner["z+"], device_id_type=MESH)
 
     plan = transfers()
     due = waits(plan)
@@ -239,10 +256,28 @@
         for number in range(len(plan)):
             if due[number] == step and plan[number][0] < step:
                 copy(number).wait_recv()
-        if step == min(t[0] for t in plan if t[1] == "z-"):
-            pl.semaphore_wait(far_sem, 1)
+        down = [n for n in range(len(plan)) if plan[n][:2] == (FIRST_Z, "z-")]
+        if step == FIRST_Z:
+
+            @pl.when(jnp.logical_not(highest))
+            def _():
+                pl.semaphore_wait(far_sem.at[0], 1)
+
+            @pl.when(jnp.logical_not(lowest))
+            def _():
+                for number in down:
+                    copy(number).start()
+
+        if step == FIRST_Z + 1:
+
+            @pl.when(lowest)
+            def _():
+                pl.semaphore_wait(far_sem.at[1], 1)
+                for number in down:
+                    copy(number).start()
+
         for number in range(len(plan)):
-            if plan[number][0] == step:
+            if plan[number][0] == step and number not in down:
                 copy(number).start()
         for number in range(len(plan)):
             if due[number] == step and plan[number][0] >= step:
@@ -388,7 +423,7 @@
             pltpu.VMEM((3, 32, targets), f32),
             pltpu.VMEM((16, targets), f32),
             pltpu.VMEM((16, targets), f32),
-            pltpu.SemaphoreType.REGULAR,
+            pltpu.SemaphoreType.REGULAR((2,)),
             pltpu.SemaphoreType.DMA((6,)),
             pltpu.SemaphoreType.DMA((count,)),
             pltpu.SemaphoreType.DMA((count,)),

time: 82.1 us -> 79.9 us (0.973); the launches traced: 80.6 us -> 79.7 us
    pallas_call x1, Pallas kernels: 77.7 us -> 76.9 us  [shards(): pl.pallas_call(forces_kernel, out_shape=jax.ShapeDtypeStruct((16, targets...]
where the time goes in v4:
time: 79.9 us; the launch traced here: 79.7 us
  Pallas kernels  76.9 us (96%)
  other arithmetic  2.11 us (3%)
    pallas_call x1, Pallas kernels, shards(): pl.pallas_call(forces_kernel, out_shape=jax.ShapeDtypeStruct((16, targets...  76.9 us

profile of v4, /device:TPU:2, one launch (start us, length us, event | category | flops | bytes accessed | tf_op | source)
XLA Modules:
  0.0 79.7 jit_solution(1689178276172504236)
XLA Ops:
  0.6 0.0 copy-start
  0.6 0.0 copy-start.1
  0.7 0.0 copy-start.2
  0.7 76.9 %shard_map.109 = f32[16,512]{1,0:T(8,128)} custom-call(f32[3,512]{1,0:T(4,128)} %pos_hbm.1, f32[3,512]{1,0:T(4,128)} %vel_hbm.1, f32[3,512]{1,0:T(4,128)} %acc_hbm.1, f32[3,512]{1,0:T(4,128)} %jerk_hbm.1, f32[3,512]{1,0:T(4,128)} %snap_hbm.1, f32[1,512]{1,0:T(1,128)} %bitcast.1), custom_call_target="tpu_custom_call" | custom-call | tf_op jit(solution)/shard_map/pallas_call | solution.py:409
  77.5 0.0 copy-done
  77.5 0.0 copy-done.1
  77.6 0.0 copy-done.2
  77.6 0.0 copy-start.3
  77.6 0.0 copy-start.4
  77.6 1.5 %multiply_add_fusion = (f32[3,512]{1,0:T(4,128)}, f32[3,512]{1,0:T(4,128)S(1)}, f32[3,512]{1,0:T(4,128)S(1)}, f32[3,512]{1,0:T(4,128)S(1)}) fusion(f32[3,512]{1,0:T(4,128)S(1)} %copy-done, f32[3,512]{1,0:T(4,128)S(1)} %copy-done.1, f32[3,512]{1,0:T(4,128)S(1)} %copy-done.2, f32[16,512]{1,0:T(8,128)} %shard_map.109), kind=kLoop, calls=%fused_computation | loop fusion | flops 21504 | bytes 61440 | tf_op jit(solution)/shard_map/add | solution.py:75
  79.1 0.0 copy-start.5
  79.1 0.0 copy-start.6
  79.1 0.0 copy-start.7
  79.1 0.0 copy-done.3
  79.1 0.0 copy-done.4
  79.1 0.6 multiply_add_fusion.1
  79.7 0.0 copy-done.5
  79.7 0.0 copy-done.6
  79.7 0.0 copy-done.7
Async XLA Ops:
  0.6 76.9 %copy-start = (f32[3,512]{1,0:T(4,128)S(1)}, f32[3,512]{1,0:T(4,128)}, u32[]{:S(2)}) copy-start(f32[3,512]{1,0:T(4,128)} %snap_hbm.1) | copy-start | bytes 18436
  0.6 76.9 %copy-start.1 = (f32[3,512]{1,0:T(4,128)S(1)}, f32[3,512]{1,0:T(4,128)}, u32[]{:S(2)}) copy-start(f32[3,512]{1,0:T(4,128)} %jerk_hbm.1) | copy-start | bytes 18436
  0.7 76.9 %copy-start.2 = (f32[3,512]{1,0:T(4,128)S(1)}, f32[3,512]{1,0:T(4,128)}, u32[]{:S(2)}) copy-start(f32[3,512]{1,0:T(4,128)} %acc_hbm.1) | copy-start | bytes 18436
  77.6 1.5 %copy-start.3 = (f32[3,512]{1,0:T(4,128)S(1)}, f32[3,512]{1,0:T(4,128)}, u32[]{:S(2)}) copy-start(f32[3,512]{1,0:T(4,128)} %pos_hbm.1) | copy-start | bytes 18436
  77.6 1.5 %copy-start.4 = (f32[3,512]{1,0:T(4,128)S(1)}, f32[3,512]{1,0:T(4,128)}, u32[]{:S(2)}) copy-start(f32[3,512]{1,0:T(4,128)} %vel_hbm.1) | copy-start | bytes 18436
  79.1 0.6 copy-start.5
  79.1 0.6 copy-start.6
  79.1 0.6 copy-start.7

commit v5 on v4

--- a/solution.py
+++ b/solution.py
@@ -399,16 +399,20 @@
     for number in range(len(plan)):
         copy(number).wait_send()
     swap.wait()
-    out_ref[...] = part[...] + other[...]
+    results = correct(
+        pos_ref[...], vel_ref[...], acc_ref[...], jerk_ref[...], snap_ref[...], part[...] + other[...]
+    )
+    for place, result in enumerate(results):
+        out_ref[place] = result
 
 
 def shards(positions, velocities, accelerations, jerks, snaps, masses):
     targets = positions.shape[1]
     half = targets // 2
     count = len(transfers())
-    forces = pl.pallas_call(
+    results = pl.pallas_call(
         forces_kernel,
-        out_shape=jax.ShapeDtypeStruct((16, targets), f32),
+        out_shape=jax.ShapeDtypeStruct((6, 3, targets), f32),
         in_specs=[pl.BlockSpec(memory_space=pltpu.HBM)] * 6,
         out_specs=pl.BlockSpec(memory_space=pltpu.VMEM),
         scratch_shapes=[pltpu.VMEM((3, targets), f32) for _ in range(5)]
@@ -433,7 +437,7 @@
             collective_id=0, has_side_effects=True, vmem_limit_bytes=60 * 2**20
         ),
     )(positions, velocities, accelerations, jerks, snaps, masses.reshape(1, targets))
-    return correct(positions, velocities, accelerations, jerks, snaps, forces)
+    return tuple(results[place] for place in range(6))
 
 
 def solution(mesh):

time: 79.9 us -> 79.2 us (level)
  other arithmetic: 2.11 us -> 0 us
  local copies, waits for them, and re-layouts: 0.04 us -> 1.41 us
    add x2 -> x0, other arithmetic: 2.11 us -> none  [the longest x1 1.49 us: correct(): crackle = 60.0 * first - 36.0 * second + 9.0 * third]
    squeeze x0 -> x1, local copies, waits for them, and re-layouts: none -> 1.41 us  [shards(): return tuple((results[place] for place in range(6)))]
where the time goes in v5:
time: 79.2 us; the launch traced here: 79 us
  Pallas kernels  76.9 us (97%)
  local copies, waits for them, and re-layouts  1.41 us (2%)
    pallas_call x1, Pallas kernels, shards(): pl.pallas_call(forces_kernel, out_shape=jax.ShapeDtypeStruct((6, 3, targe...  76.9 us

profile of v5, /device:TPU:2, one launch (start us, length us, event | category | flops | bytes accessed | tf_op | source)
XLA Modules:
  0.0 79.0 jit_solution(3057349328131176199)
XLA Ops:
  0.6 76.9 %shard_map.109 = f32[6,3,512]{2,1,0:T(4,128)} custom-call(f32[3,512]{1,0:T(4,128)} %pos_hbm.1, f32[3,512]{1,0:T(4,128)} %vel_hbm.1, f32[3,512]{1,0:T(4,128)} %acc_hbm.1, f32[3,512]{1,0:T(4,128)} %jerk_hbm.1, f32[3,512]{1,0:T(4,128)} %snap_hbm.1, f32[1,512]{1,0:T(1,128)} %bitcast.13), custom_call_target="tpu_custom_call" | custom-call | tf_op jit(solution)/shard_map/pallas_call | solution.py:413
  77.6 1.4 %slice_bitcast_fusion = (f32[3,512]{1,0:T(4,128)}, f32[3,512]{1,0:T(4,128)}, f32[3,512]{1,0:T(4,128)}, f32[3,512]{1,0:T(4,128)}, f32[3,512]{1,0:T(4,128)}, /*index=5*/f32[3,512]{1,0:T(4,128)}) fusion(f32[6,3,512]{2,1,0:T(4,128)} %shard_map.109), kind=kLoop, calls=%fused_computation | loop fusion | bytes 73728 | tf_op jit(solution)/shard_map/squeeze | solution.py:440
